TPU v7x, 512 devices: a whole 4x8x8 slice. The times are simulated.
512 devices in a mesh: group: 16 (over y, core), seq: 32 (over x, z).
Axes of the slice: x: 4, y: 8, z: 8, core: 2. Of those that a mesh axis runs over, the one named last changes fastest.
Arguments:
- cand_x: bfloat16 [65536, 1024], P(('group', 'seq')), may hold values from -6 to 6
- in_weight: bfloat16 [1024, 4096], P(None, 'group'), may hold values from -0.1875 to 0.1875
- out_weight: bfloat16 [1024, 1024], P('group'), may hold values from -0.1875 to 0.1875
- in_gain: float32 [1024], replicated, may hold values from 0.25 to 1.75
- out_gain: float32 [1024], replicated, may hold values from 0.25 to 1.75
- cache_kv: bfloat16 [2, 128, 2048, 1024], P(None, 'group', 'seq'), may hold values from -6 to 6
- hist_len: int32 [128], P('group'), may hold values from 128 to 2048, as said below
- owner: int32 [16, 32], P('group'), may hold values from 0 to 7, as said below
Outputs:
- mixed: bfloat16 [65536, 1024], P(('group', 'seq'))
Inputs may be any that keep to these rules, and one draw needn't show every extreme that they name: `hist_len`: multiples of 128; some request has all 2048 slots live. `owner`: in each group every request index appears exactly four times.
All inputs are finite; a program needn't handle non-finite values.
Results may differ from a plain program's by a relative error of at most 0.0056.
Values may be sent and summed in bfloat16 or wider, within the bound.
A program may use at most 128 MiB of HBM per device.

v0:
```python
import math

import jax
import jax.numpy as jnp
from jax import lax
from jax.sharding import PartitionSpec as P

HEADS = 8


def layer_norm(values_in, gain):
    values_in = values_in.astype(jnp.float32)
    centre = jnp.mean(values_in, axis=-1, keepdims=True)
    centred = values_in - centre
    spread = jnp.mean(centred * centred, axis=-1, keepdims=True)
    return centred * lax.rsqrt(spread + 1e-05) * gain


def local(cand_x, in_weight, out_weight, in_gain, out_gain, cache_kv, hist_len, owner):
    row_count, model_width = cand_x.shape
    head_size = model_width // HEADS
    factor = 1.0 / math.sqrt(head_size)
    normed = layer_norm(cand_x, in_gain).astype(jnp.bfloat16)
    gathered = lax.all_gather(normed, "group", axis=0, tiled=True)
    partial_value = jax.nn.silu(
        jnp.dot(gathered, in_weight, preferred_element_type=jnp.float32)
    ).astype(jnp.bfloat16)
    project = lax.all_to_all(partial_value, "group", split_axis=0, concat_axis=1, tiled=True)
    targets = owner[0]
    outgoing = jnp.take(cache_kv, targets, axis=1)
    incoming = lax.all_to_all(outgoing, "seq", split_axis=1, concat_axis=2, tiled=True)
    key_heads = incoming[0, 0].reshape(-1, HEADS, head_size)
    value_heads = incoming[1, 0].reshape(-1, HEADS, head_size)
    history_len = key_heads.shape[0]
    request = lax.dynamic_index_in_dim(targets, lax.axis_index("seq"), 0, keepdims=False)
    request_ids = jnp.arange(hist_len.shape[0], dtype=jnp.int32)
    length = jnp.sum(jnp.where(request_ids == request, hist_len, 0))
    gate_u = project[:, :model_width]
    own_v = project[:, model_width : 2 * model_width].reshape(row_count, HEADS, head_size)
    query = project[:, 2 * model_width : 3 * model_width].reshape(row_count, HEADS, head_size)
    own_k = project[:, 3 * model_width :].reshape(row_count, HEADS, head_size)
    scores = (
        jnp.einsum("qhd,khd->hqk", query, key_heads, preferred_element_type=jnp.float32) * factor
    )
    live = (jnp.arange(history_len, dtype=jnp.int32) < length).astype(jnp.float32)
    weights = (jax.nn.silu(scores) * live[None, None, :]).astype(jnp.bfloat16)
    attended = jnp.einsum("hqk,khd->qhd", weights, value_heads, preferred_element_type=jnp.float32)
    own_score = jnp.sum(query.astype(jnp.float32) * own_k.astype(jnp.float32), axis=-1) * factor
    attended = attended + jax.nn.silu(own_score)[:, :, None] * own_v.astype(jnp.float32)
    gated = (
        layer_norm(attended.reshape(row_count, model_width), out_gain) * gate_u.astype(jnp.float32)
    ).astype(jnp.bfloat16)
    projected = jnp.dot(
        gated,
        lax.all_gather(out_weight, "group", axis=0, tiled=True),
        preferred_element_type=jnp.float32,
    )
    return (cand_x.astype(jnp.float32) + projected).astype(jnp.bfloat16)


def solution(mesh):
    placed = (
        P(("group", "seq"), None),
        P(None, "group"),
        P("group", None),
        P(),
        P(),
        P(None, "group", "seq", None),
        P("group"),
        P("group", None),
    )
    return jax.shard_map(
        local, mesh=mesh, in_specs=placed, out_specs=P(("group", "seq"), None), check_vma=False
    )
```

profile of v0, /device:TPU:221, one launch (start us, length us, event | category | flops | bytes accessed | tf_op | source)
XLA Modules:
  0.0 337.6 jit_solution(11690608931788743895)
XLA Ops:
  6.5 0.0 copy-start
  6.5 0.0 all-gather.3.cloned.1.call-start
  6.5 1.2 convert_reduce_fusion
  7.8 1.2 fusion.14
  8.9 1.9 fusion.16
  10.8 0.0 all-gather.3.cloned.1.call-update
  10.9 46.8 %all-gather.3.cloned.1.call-done = bf16[2048,1024]{1,0:T(8,128)(2,1)} async-done(((bf16[128,1024]{1,0:T(8,128)(2,1)}), bf16[2048,1024]{1,0:T(8,128)(2,1)}) %all-gather.3.cloned.1.call-update) | async-done | bytes 4194320 | tf_op jit(solution)/shard_map/all_gather | solution.py:24
  57.6 3.7 %multiply_convert_fusion.1 = bf16[2048,256]{1,0:T(8,128)(2,1)S(1)} fusion(bf16[2048,1024]{1,0:T(8,128)(2,1)} %all-gather.3.cloned.1.call-done, bf16[1024,256]{1,0:T(8,128)(2,1)} %param.9), kind=kOutput, calls=%fused_computation.6 | convolution fusion | flops 1076363264 | bytes 5767168 | tf_op jit(solution)/shard_map/dot_general | solution.py:26
  61.3 0.0 copy-start.3
  61.3 1.3 copy.10
  62.6 5.6 %all-to-all-start.1 = ((bf16[16,128,256]{1,2,0:T(8,128)(2,1)}), bf16[16,128,256]{1,2,0:T(8,128)(2,1)S(1)}, u32[]{:S(2)}, u32[]{:S(2)}) async-start(bf16[16,128,256]{1,2,0:T(8,128)(2,1)} %copy.10), calls=%async_computation.1 | async-start | bytes 2097152 | tf_op jit(solution)/shard_map/all_to_all | solution.py:28
  68.2 0.0 copy-done.3
  68.2 0.0 copy-done
  68.2 5.0 %gather_fusion = bf16[32,2,64,1024]{3,2,1,0:T(8,128)(2,1)} fusion(bf16[2,8,64,1024]{3,2,1,0:T(8,128)(2,1)S(1)} %copy-done, s32[1024]{0:T(1024)S(1)} %pad_clamp_fusion), kind=kCustom, calls=%fused_computation | custom fusion | bytes 16777344 | tf_op jit(solution)/shard_map/jit(_take)/gather | solution.py:30
  73.2 7.5 %select_bitcast_fusion = bf16[2,32,64,1024]{3,2,0,1:T(8,128)(2,1)} fusion(bf16[32,2,64,1024]{3,2,1,0:T(8,128)(2,1)} %gather_fusion, pred[32]{0:T(512)(128)(4,1)S(1)} %compare_and_fusion), kind=kLoop, calls=%fused_computation.1 | loop fusion | flops 4194304 | bytes 16777248 | tf_op jit(solution)/shard_map/jit(_take)/select_n | solution.py:30
  80.7 0.0 copy-start.4
  80.7 13.7 %all-to-all-done.1 = bf16[16,128,256]{1,2,0:T(8,128)(2,1)S(1)} async-done(((bf16[16,128,256]{1,2,0:T(8,128)(2,1)}), bf16[16,128,256]{1,2,0:T(8,128)(2,1)S(1)}, u32[]{:S(2)}, u32[]{:S(2)}) %all-to-all-start.1) | async-done | bytes 1048608 | tf_op jit(solution)/shard_map/all_to_all | solution.py:28
  94.4 9.5 %all-to-all-start = ((bf16[2,32,64,1024]{3,2,0,1:T(8,128)(2,1)}), bf16[2,32,64,1024]{3,2,0,1:T(8,128)(2,1)}, u32[]{:S(2)}, u32[]{:S(2)}) async-start(bf16[2,32,64,1024]{3,2,0,1:T(8,128)(2,1)} %select_bitcast_fusion), calls=%async_computation | async-start | bytes 16777216 | tf_op jit(solution)/shard_map/all_to_all | solution.py:31
  103.8 0.2 all-gather.5.cloned.1.call-start
  104.1 0.5 all-gather.5.cloned.1.call-update
  104.6 0.6 constant_dynamic-slice_fusion
  105.2 0.0 copy-done.4
  105.2 1.3 fusion.23
  106.5 0.6 fusion.22
  107.1 0.9 fusion.28
  108.0 0.1 fusion.17
  108.1 197.6 %all-to-all-done = bf16[2,32,64,1024]{3,2,0,1:T(8,128)(2,1)} async-done(((bf16[2,32,64,1024]{3,2,0,1:T(8,128)(2,1)}), bf16[2,32,64,1024]{3,2,0,1:T(8,128)(2,1)}, u32[]{:S(2)}, u32[]{:S(2)}) %all-to-all-start) | async-done | bytes 8388640 | tf_op jit(solution)/shard_map/all_to_all | solution.py:31
  305.7 3.9 %fusion.27 = (bf16[1,32,64,1024]{3,2,0,1:T(8,128)(2,1)S(1)}, bf16[1,32,64,1024]{3,2,0,1:T(8,128)(2,1)S(1)}) fusion(bf16[2,32,64,1024]{3,2,0,1:T(8,128)(2,1)} %all-to-all-done), kind=kLoop, calls=%fused_computation.44 | loop fusion | bytes 16777216 | tf_op jit(solution)/shard_map/slice | solution.py:32
  309.6 3.0 copy.16
  312.6 3.1 copy.15
  315.7 0.0 copy-start.2
  315.7 0.0 copy-start.1
  315.7 9.0 %fusion.29 = (f32[128]{0:T(128)S(1)}, f32[128,8,128]{0,2,1:T(8,128)}) fusion(bf16[128,8,128]{0,2,1:T(8,128)(2,1)} %bitcast.57, f32[128,8]{0,1:T(8,128)S(1)} %divide_multiply_fusion, bf16[128,8,128]{0,2,1:T(8,128)(2,1)} %bitcast.58, bf16[2048,8,128]{2,1,0:T(8,128)(2,1)} %bitcast.54, f32[2048]{0:T(1024)S(1)} %fusion.22, bf16[2048,8,128]{2,1,0:T(8,128)(2,1)} %bitcast.55), kind=kOutput, calls=%fused_computation.46 | convolution fusion | flops 1088946048 | bytes 9449984 | tf_op jit(solution)/shard_map/hqk,khd->qhd/dot_general | solution.py:47
  324.7 1.2 multiply_reduce_fusion
  325.9 0.0 copy-done.2
  325.9 2.0 fusion.21
  327.9 0.0 all-gather.5.cloned.1.call-done
  327.9 0.0 copy-done.1
  327.9 2.9 fusion.9
  (8 shorter events, 0.1 us)
Async XLA Ops:
  6.5 61.7 %copy-start = (bf16[2,8,64,1024]{3,2,1,0:T(8,128)(2,1)S(1)}, bf16[2,8,64,1024]{3,2,1,0:T(8,128)(2,1)}, u32[]{:S(2)}) copy-start(bf16[2,8,64,1024]{3,2,1,0:T(8,128)(2,1)} %param.13) | copy-start | bytes 6291460
  6.5 51.1 %all-gather.3.cloned.1.call-start = ((), (), s32[]{:S(2)}) async-start(), calls=%async_computation.2 | async-start | bytes 4456448 | tf_op jit(solution)/shard_map/all_gather | solution.py:24
  61.3 6.9 %copy-start.3 = (s32[1,32]{1,0:T(1,128)S(1)}, s32[1,32]{1,0:T(1,128)}, u32[]{:S(2)}) copy-start(s32[1,32]{1,0:T(1,128)} %param.15) | copy-start | bytes 388
  62.6 31.8 %all-to-all-start.1 = ((bf16[16,128,256]{1,2,0:T(8,128)(2,1)}), bf16[16,128,256]{1,2,0:T(8,128)(2,1)S(1)}, u32[]{:S(2)}, u32[]{:S(2)}) async-start(bf16[16,128,256]{1,2,0:T(8,128)(2,1)} %copy.10), calls=%async_computation.1 | async-start | bytes 2097152 | tf_op jit(solution)/shard_map/all_to_all | solution.py:28
  80.7 24.5 %copy-start.4 = (s32[8]{0:T(128)S(1)}, s32[8]{0:T(128)}, u32[]{:S(2)}) copy-start(s32[8]{0:T(128)} %param.14) | copy-start | bytes 100
  94.4 211.3 %all-to-all-start = ((bf16[2,32,64,1024]{3,2,0,1:T(8,128)(2,1)}), bf16[2,32,64,1024]{3,2,0,1:T(8,128)(2,1)}, u32[]{:S(2)}, u32[]{:S(2)}) async-start(bf16[2,32,64,1024]{3,2,0,1:T(8,128)(2,1)} %select_bitcast_fusion), calls=%async_computation | async-start | bytes 16777216 | tf_op jit(solution)/shard_map/all_to_all | solution.py:31
  103.8 224.0 %all-gather.5.cloned.1.call-start = ((), (), s32[]{:S(2)}) async-start(), calls=%async_computation.3 | async-start | bytes 2228224 | tf_op jit(solution)/shard_map/all_gather | solution.py:55
  315.7 10.2 %copy-start.2 = (f32[1024]{0:T(1024)S(1)}, f32[1024]{0:T(1024)}, u32[]{:S(2)}) copy-start(f32[1024]{0:T(1024)} %param.12) | copy-start | bytes 12292
  315.7 12.2 %copy-start.1 = (bf16[128,1024]{1,0:T(8,128)(2,1)S(1)}, bf16[128,1024]{1,0:T(8,128)(2,1)}, u32[]{:S(2)}) copy-start(bf16[128,1024]{1,0:T(8,128)(2,1)} %param.8) | copy-start | bytes 786436
Sparse Core Ops, SparseCore 0:
  11.0 46.5 all-gather.2
  106.8 41.5 all-gather.4
where the time goes:
time: 338 us
  waiting for transfers between devices  259 us (77%)
  local copies, waits for them, and re-layouts  17.8 us (5%)
  other arithmetic  16.9 us (5%)
  matrix products  15.5 us (5%)
  starting transfers between devices  15.2 us (4%)
  between operations  13.5 us (4%)
    all_to_all x1, waiting for transfers between devices, local(): lax.all_to_all(outgoing, 'seq', split_axis=1, concat_axis=2, tiled=True)  198 us
    all_gather x1, waiting for transfers between devices, local(): gathered = lax.all_gather(normed, 'group', axis=0, tiled=True)  46.8 us
    all_to_all x1, waiting for transfers between devices, local(): lax.all_to_all(partial_value, 'group', split_axis=0, concat_axis=1, tiled...  13.7 us
    all_to_all x1, starting transfers between devices, local(): lax.all_to_all(outgoing, 'seq', split_axis=1, concat_axis=2, tiled=True)  9.45 us
    dot_general x1, matrix products, local(): jnp.einsum('hqk,khd->qhd', weights, value_heads, preferred_element_type=j...  9.01 us
    select_n x2, other arithmetic, local(): outgoing = jnp.take(cache_kv, targets, axis=1)  7.46 us
  transfers between devices with their start and end apart: 4, of which 3 were waited for; matrix products, arithmetic and copies ran while one was open for 11% of the time, Pallas kernels for 0%

commit v1 on v0

v1 whole, which is shorter than its diff:
```python
import math

import jax
import jax.numpy as jnp
from jax import lax
from jax.experimental import pallas as pl
from jax.experimental.pallas import tpu as pltpu
from jax.sharding import PartitionSpec as P

HEADS = 8
HEAD = 128
NY, NX, NZ = 8, 4, 8
QSPLIT = 4
ROWS = 128
D = 1024
BLOCK = 256
SLOTS = 64
REQ = 8


def silu(v):
    half = 0.5 * v
    return half + half * jnp.tanh(half)


def layer_norm(values_in, gain):
    centre = jnp.mean(values_in, axis=-1, keepdims=True)
    centred = values_in - centre
    spread = jnp.mean(centred * centred, axis=-1, keepdims=True)
    return centred * lax.rsqrt(spread + 1e-05) * gain


def kernel(cand_ref, inw_ref, outw_ref, ing_ref, outg_ref, cache_ref, len_ref, owner_ref, out_ref, *scratch):
    kvs = scratch[:HEADS]
    (win, wout, nbuf, qbuf, ubuf, snd, rcv, acc,
     lk, lw, xs, xr, zs, zr, qs, qr, qcs, qcr, ys, yr, ycs, ycr, ss, rs) = scratch[HEADS:]
    g = lax.axis_index("group")
    s = lax.axis_index("seq")
    y, c = g // 2, g % 2
    x, z = s // NZ, s % NZ
    factor = 1.0 / math.sqrt(HEAD)

    def at_y(yy):
        return {"group": lax.rem(yy + NY, NY) * 2 + c}

    def at_x(xx):
        return {"seq": lax.rem(xx + NX, NX) * NZ + z}

    def at_z(zz):
        return {"seq": x * NZ + lax.rem(zz + NZ, NZ)}

    partner = {"group": y * 2 + 1 - c}
    y_peer = (at_y(y + 1), at_y(y - 1))
    x_peer = (at_x(x + 1), at_x(x - 1))
    z_peer = (at_z(z + 1), at_z(z - 1))

    def remote(src, dst, send, recv, device):
        return pltpu.make_async_remote_copy(src, dst, send, recv, device_id=device, device_id_type=pl.DeviceIdType.MESH)

    def local_kv(h):
        return pltpu.make_async_copy(
            cache_ref.at[:, :, :, pl.ds(h * HEAD, HEAD)], kvs[h].at[:, :, x], lk.at[h]
        )

    own_win = pltpu.make_async_copy(inw_ref, win.at[g], lw.at[0])
    own_wout = pltpu.make_async_copy(outw_ref, wout.at[g], lw.at[1])
    for h in range(HEADS):
        local_kv(h).start()
    own_win.start()
    own_wout.start()

    barrier = pltpu.get_barrier_semaphore()
    for peer in (partner,) + y_peer + x_peer + tuple(at_z(z + k) for k in range(1, NZ)):
        pl.semaphore_signal(barrier, inc=1, device_id=peer, device_id_type=pl.DeviceIdType.MESH)

    nbuf[pl.ds(pl.multiple_of(z * ROWS, ROWS), ROWS), :] = layer_norm(
        cand_ref[...].astype(jnp.float32), ing_ref[...]
    ).astype(jnp.bfloat16)
    for h in range(HEADS):
        local_kv(h).wait()
    own_win.wait()
    own_wout.wait()
    pl.semaphore_wait(barrier, 5 + NZ - 1)

    def x_first(h, way):
        ref = kvs[h].at[:, :, x]
        return remote(ref, ref, xs.at[h, way], xr.at[h, way], x_peer[way])

    def x_second(h, way):
        block = lax.rem(x + (NX - 1 if way == 0 else 1), NX)
        ref = kvs[h].at[way, :, block]
        return remote(ref, ref, xs.at[h, 2 + way], xr.at[h, 2 + way], x_peer[way])

    def x_handle(h):
        for way in range(2):
            block = lax.rem(x + (NX - 1 if way == 0 else 1), NX)
            ref = kvs[h].at[:, :, block]
            remote(ref, ref, xs.at[h, way], xr.at[h, way], x_peer[way]).wait_recv()
            x_second(h, way).start()
        if h + 2 < HEADS:
            for way in range(2):
                x_first(h + 2, way).start()

    def x_complete(h):
        block = lax.rem(x + 2, NX)
        for way in range(2):
            ref = kvs[h].at[way, :, block]
            remote(ref, ref, xs.at[h, 2 + way], xr.at[h, 2 + way], x_peer[way]).wait_recv()

    def z_copy(hop, part, way):
        block = lax.rem(z + (NZ - hop if way == 0 else hop), NZ)
        start = pl.multiple_of(block * ROWS + part * (ROWS // 2), ROWS // 2)
        ref = nbuf.at[pl.ds(start, ROWS // 2), :]
        return remote(ref, ref, zs.at[min(hop, 3), part, way], zr.at[min(hop, 3), part, way], z_peer[way])

    def z_arrival(hop, part, way):
        block = lax.rem(z + (NZ - hop if way == 0 else hop), NZ)
        start = pl.multiple_of(block * ROWS + part * (ROWS // 2), ROWS // 2)
        ref = nbuf.at[pl.ds(start, ROWS // 2), :]
        return remote(ref, ref, zs.at[hop - 1, part, way], zr.at[hop - 1, part, way], z_peer[way])

    def z_sends(hop, part, way):
        return hop < 3 or (hop == 3 and part == way)

    def z_handle(hop, part):
        for way in range(2):
            if hop < 4 or part == way:
                z_arrival(hop, part, way).wait_recv()
            if z_sends(hop, part, way):
                z_copy(hop, part, way).start()

    QROWS = D // QSPLIT

    def q_ref(b, part, core):
        return win.at[2 * b + core, pl.ds(part * QROWS, QROWS), :]

    def q_right(b, part):
        d = lax.rem(y - b + NY, NY)
        return (d <= 2) | (d == 3) if part < QSPLIT // 2 else d <= 2

    def q_left(b, part):
        e = lax.rem(b - y + NY, NY)
        return (e <= 2) | (e == 3) if part >= QSPLIT // 2 else e <= 2

    def q_copy(b, part, way):
        ref = q_ref(b, part, c)
        return remote(ref, ref, qs.at[b - 4, part, way], qr.at[b - 4, part], y_peer[way])

    def q_cross(b, part):
        ref = q_ref(b, part, c)
        return remote(ref, ref, qcs.at[b - 4, part], qcr.at[b - 4, part], partner)

    def q_handle(b, part):
        @pl.when(y != b)
        def _():
            q_copy(b, part, 0).wait_recv()

        @pl.when(q_right(b, part))
        def _():
            q_copy(b, part, 0).start()

        @pl.when(q_left(b, part))
        def _():
            q_copy(b, part, 1).start()

        q_cross(b, part).start()

    def q_cross_arrival(b, part):
        ref = q_ref(b, part, 1 - c)
        remote(ref, ref, qcs.at[b - 4, part], qcr.at[b - 4, part], partner).wait_recv()

    def w_ref(block, piece):
        if piece == 2:
            return wout.at[block]
        return win.at[block, pl.ds(piece * (D // 2), D // 2), :]

    def y_block(hop, way):
        return lax.rem(y + (NY - hop if way == 0 else hop), NY)

    def y_guard(hop, piece, way):
        b = y_block(hop, way)
        return (b != 4) & (b != 5) if piece < 2 else y >= 0

    def y_sends(hop, piece, way):
        return hop < 3 or (hop == 3 and (piece == 1) == (way == 1))

    def y_copy(hop, piece, way):
        ref = w_ref(2 * y_block(hop, way) + c, piece)
        return remote(ref, ref, ys.at[hop, piece, way], yr.at[hop, piece, way], y_peer[way])

    def y_arrival(hop, piece, way):
        ref = w_ref(2 * y_block(hop, way) + c, piece)
        return remote(ref, ref, ys.at[hop - 1, piece, way], yr.at[hop - 1, piece, way], y_peer[way])

    def y_cross(b, piece):
        ref = w_ref(2 * b + c, piece)
        return remote(ref, ref, ycs.at[b, piece], ycr.at[b, piece], partner)

    def y_cross_arrival(b, piece):
        ref = w_ref(2 * b + 1 - c, piece)
        remote(ref, ref, ycs.at[b, piece], ycr.at[b, piece], partner).wait_recv()

    def y_handle(hop, piece):
        for way in range(2):
            if hop == 4 and (piece == 1) != (way == 1):
                continue

            @pl.when(y_guard(hop, piece, way))
            def _():
                y_arrival(hop, piece, way).wait_recv()
                if y_sends(hop, piece, way):
                    y_copy(hop, piece, way).start()
                y_cross(y_block(hop, way), piece).start()

    early = ((y <= 3), (y <= 1) | (y >= 6))

    def y_own(first):
        for piece in range(3):
            for way in range(2):
                chosen = early[way] if first else jnp.logical_not(early[way])

                @pl.when(chosen & y_guard(0, piece, way))
                def _():
                    y_copy(0, piece, way).start()

    def queries(block):
        @pl.loop(0, NZ // 2)
        def _(i):
            rows = pl.ds(pl.multiple_of(i * 2 * ROWS, 2 * ROWS), 2 * ROWS)
            value = jnp.dot(nbuf[rows, :], win[2 * 4 + block], preferred_element_type=jnp.float32)
            qbuf[rows, block * BLOCK : (block + 1) * BLOCK] = silu(value).astype(jnp.bfloat16)

    column = lax.broadcasted_iota(jnp.int32, (1, NX * SLOTS), 1)
    slot = (column // SLOTS * NZ + z) * SLOTS + column % SLOTS

    def send_partial(h, dest):
        return remote(snd.at[h, dest], rcv.at[h, z], ss.at[h, dest], rs.at[h, z], at_z(dest))

    def attend(h):
        kv = kvs[h]

        @pl.loop(0, NZ)
        def _(i):
            step = (i + 1) // 2
            dest = lax.rem(z + 4 + NZ + (1 - 2 * (i % 2)) * step, NZ)
            request = owner_ref[0, x * NZ + dest]
            length = len_ref[request]
            query = qbuf[pl.ds(pl.multiple_of(dest * ROWS, ROWS), ROWS), h * HEAD : (h + 1) * HEAD]
            keys = kv[0, request].reshape(NX * SLOTS, HEAD)
            values = kv[1, request].reshape(NX * SLOTS, HEAD)
            scores = lax.dot_general(
                query, keys, (((1,), (1,)), ((), ())), preferred_element_type=jnp.float32
            )
            weights = jnp.where(slot < length, silu(scores * factor), 0.0).astype(jnp.bfloat16)
            part = jnp.dot(weights, values, preferred_element_type=jnp.float32)
            snd[h, dest] = part.astype(jnp.bfloat16)

            @pl.when(i < NZ - 1)
            def _():
                send_partial(h, dest).start()

    def collect(h):
        total = acc[:, h * HEAD : (h + 1) * HEAD] + snd[h, z].astype(jnp.float32)
        for k in range(1, NZ):
            src = lax.rem(z + k, NZ)
            remote(snd.at[h, src], rcv.at[h, src], ss.at[h, src], rs.at[h, src], at_z(src)).wait_recv()
            total = total + rcv[h, src].astype(jnp.float32)
        acc[:, h * HEAD : (h + 1) * HEAD] = total

    def own_rows():
        rows = pl.ds(pl.multiple_of(z * ROWS, ROWS), ROWS)
        mine = nbuf[rows, :]

        def project(block):
            value = jnp.dot(mine, win[block], preferred_element_type=jnp.float32)
            return silu(value).astype(jnp.bfloat16)

        for j in range(4):
            columns = slice(j * BLOCK, (j + 1) * BLOCK)
            ubuf[:, columns] = project(j)
            own_v = project(4 + j).astype(jnp.float32)
            own_k = project(12 + j).astype(jnp.float32)
            product = qbuf[rows, columns].astype(jnp.float32) * own_k
            for t in range(BLOCK // HEAD):
                part = slice(t * HEAD, (t + 1) * HEAD)
                score = jnp.sum(product[:, part], axis=-1, keepdims=True) * factor
                acc[:, j * BLOCK + t * HEAD : j * BLOCK + (t + 1) * HEAD] = silu(score) * own_v[:, part]

    for h in range(2):
        for way in range(2):
            x_first(h, way).start()
    for part in range(2):
        for way in range(2):
            z_copy(0, part, way).start()
    y_own(True)
    for piece in range(3):
        @pl.when(y_guard(0, piece, 0))
        def _():
            y_cross(y, piece).start()

    for i in range(8):
        q_handle(4 + i // QSPLIT, i % QSPLIT)
        z_handle(1 + i // 2, i % 2)
        if i in (2, 5):
            x_handle(i // 3)
    y_own(False)
    for part in range(QSPLIT):
        q_cross_arrival(4, part)
    queries(0)
    queries(1)
    x_handle(2)
    x_complete(0)
    attend(0)
    x_complete(1)
    attend(1)
    for piece in range(3):
        y_handle(1, piece)
    x_handle(3)
    x_complete(2)
    attend(2)
    for part in range(QSPLIT):
        q_cross_arrival(5, part)
    queries(2)
    queries(3)
    for piece in range(3):
        y_handle(2, piece)
    x_handle(4)
    x_complete(3)
    attend(3)
    for piece in range(3):
        y_handle(3, piece)
    x_handle(5)
    x_complete(4)
    attend(4)
    for piece in range(3):
        y_handle(4, piece)
    x_handle(6)
    x_complete(5)
    attend(5)
    for b in range(NY):
        if b not in (4, 5):
            y_cross_arrival(b, 0)
            y_cross_arrival(b, 1)
    own_rows()
    x_handle(7)
    x_complete(6)
    attend(6)
    for h in range(6):
        collect(h)
    x_complete(7)
    attend(7)
    for b in range(NY):
        y_cross_arrival(b, 2)
    collect(6)
    collect(7)
    gated = (layer_norm(acc[...], outg_ref[...]) * ubuf[...].astype(jnp.float32)).astype(jnp.bfloat16)
    result = jnp.dot(gated, wout[...].reshape(D, D), preferred_element_type=jnp.float32)
    out_ref[...] = (cand_ref[...].astype(jnp.float32) + result).astype(jnp.bfloat16)

    for h in range(HEADS):
        for way in range(2):
            x_first(h, way).wait_send()
            x_second(h, way).wait_send()
    for hop in range(4):
        for part in range(2):
            for way in range(2):
                if z_sends(hop, part, way):
                    z_copy(hop, part, way).wait_send()
    for b in (4, 5):
        for part in range(QSPLIT):
            q_cross(b, part).wait_send()

            @pl.when(q_right(b, part))
            def _():
                q_copy(b, part, 0).wait_send()

            @pl.when(q_left(b, part))
            def _():
                q_copy(b, part, 1).wait_send()

    for piece in range(3):
        for hop in range(4):
            for way in range(2):
                if y_sends(hop, piece, way):
                    @pl.when(y_guard(hop, piece, way))
                    def _():
                        y_copy(hop, piece, way).wait_send()
        for b in range(NY):
            if piece == 2 or b not in (4, 5):
                y_cross(b, piece).wait_send()

    for h in range(HEADS):
        @pl.loop(1, NZ)
        def _(k):
            send_partial(h, lax.rem(z + k, NZ)).wait_send()


def local(cand_x, in_weight, out_weight, in_gain, out_gain, cache_kv, hist_len, owner):
    bf16, dma = jnp.bfloat16, pltpu.SemaphoreType.DMA
    vmem, anywhere = pl.BlockSpec(memory_space=pltpu.VMEM), pl.BlockSpec(memory_space=pl.ANY)
    smem = pl.BlockSpec(memory_space=pltpu.SMEM)
    return pl.pallas_call(
        kernel,
        out_shape=jax.ShapeDtypeStruct((ROWS, D), bf16),
        in_specs=[vmem, anywhere, anywhere, vmem, vmem, anywhere, smem, smem],
        out_specs=vmem,
        scratch_shapes=[pltpu.VMEM((2, REQ, NX, SLOTS, HEAD), bf16) for _ in range(HEADS)]
        + [
            pltpu.VMEM((2 * NY, D, BLOCK), bf16),
            pltpu.VMEM((2 * NY, D // (2 * NY), D), bf16),
            pltpu.VMEM((NZ * ROWS, D), bf16),
            pltpu.VMEM((NZ * ROWS, D), bf16),
            pltpu.VMEM((ROWS, D), bf16),
            pltpu.VMEM((HEADS, NZ, ROWS, HEAD), bf16),
            pltpu.VMEM((HEADS, NZ, ROWS, HEAD), bf16),
            pltpu.VMEM((ROWS, D), jnp.float32),
            dma((HEADS,)), dma((2,)),
            dma((HEADS, 4)), dma((HEADS, 4)),
            dma((4, 2, 2)), dma((4, 2, 2)),
            dma((2, QSPLIT, 2)), dma((2, QSPLIT)), dma((2, QSPLIT)), dma((2, QSPLIT)),
            dma((4, 3, 2)), dma((4, 3, 2)), dma((NY, 3)), dma((NY, 3)),
            dma((HEADS, NZ)), dma((HEADS, NZ)),
        ],
        compiler_params=pltpu.CompilerParams(
            collective_id=0, has_side_effects=True, vmem_limit_bytes=56 * 1024 * 1024
        ),
        cost_estimate=pl.CostEstimate(flops=5_000_000_000, bytes_accessed=4_000_000, transcendentals=4_000_000),
    )(cand_x, in_weight, out_weight, in_gain[None, :], out_gain[None, :], cache_kv, hist_len, owner)


def solution(mesh):
    placed = (
        P(("group", "seq"), None),
        P(None, "group"),
        P("group", None),
        P(),
        P(),
        P(None, "group", "seq", None),
        P("group"),
        P("group", None),
    )
    return jax.shard_map(
        local, mesh=mesh, in_specs=placed, out_specs=P(("group", "seq"), None), check_vma=False
    )
```

time: 338 us -> 124 us (0.37)
  the two profiles are of different devices: /device:TPU:221 before, /device:TPU:6 now
where the time goes in v1:
time: 124 us; the launch traced here: 122 us
  Pallas kernels  120 us (97%)
  local copies, waits for them, and re-layouts  1.67 us (1%)
    pallas_call x1, Pallas kernels, local(): pl.pallas_call(kernel, out_shape=jax.ShapeDtypeStruct((ROWS, D), bf16), i...  120 us

profile of v1, /device:TPU:6, one launch (start us, length us, event | category | flops | bytes accessed | tf_op | source)
XLA Modules:
  0.0 121.8 jit_solution(6328294478470404581)
XLA Ops:
  0.0 120.1 %shard_map.82 = bf16[128,1024]{1,0:T(8,128)(2,1)} custom-call(bf16[128,1024]{1,0:T(8,128)(2,1)} %cand_ref.1, bf16[1024,256]{1,0:T(8,128)(2,1)} %inw_ref.1, bf16[64,1024]{1,0:T(8,128)(2,1)} %outw_ref.1, f32[1,1024]{1,0:T(1,128)} %bitcast.2, f32[1,1024]{1,0:T(1,128)} %bitcast.3, bf16[2,8,64,1024]{3,2,1,0:T(8,128)(2,1)} %cache_ref.1, s32[8]{0:T(128)} %len_ref.1, ...), custom_call_target="tpu_custom_call" | custom-call | flops 5000000000 | bytes 4000000 | tf_op jit(solution)/shard_map/pallas_call | solution.py:402
  120.1 1.7 %copy.10 = bf16[128,1024]{1,0:T(8,128)(2,1)} copy(bf16[128,1024]{1,0:T(8,128)(2,1)} %shard_map.82) | data formatting | bytes 524288

commit v2 on v1

v2 whole, which is shorter than its diff:
```python
import math

import jax
import jax.numpy as jnp
from jax import lax
from jax.experimental import pallas as pl
from jax.experimental.pallas import tpu as pltpu
from jax.sharding import PartitionSpec as P

HEADS = 8
HEAD = 128
NY, NX, NZ = 8, 4, 8
PIECES = 2
ROWS = 128
D = 1024
BLOCK = 256
SLOTS = 64
REQ = 8
PIECE = D // PIECES
WINDOW = 2
UNROLL = 2
RING = 6


def silu(v):
    half = 0.5 * v
    return half + half * jnp.tanh(half)


def layer_norm(values_in, gain):
    centre = jnp.mean(values_in, axis=-1, keepdims=True)
    centred = values_in - centre
    spread = jnp.mean(centred * centred, axis=-1, keepdims=True)
    return centred * lax.rsqrt(spread + 1e-05) * gain


def kernel(cand_ref, inw_ref, outw_ref, ing_ref, outg_ref, cache_ref, len_ref, owner_ref, out_ref, *scratch):
    kvs = scratch[:HEADS]
    (win, wout, nbuf, qbuf, ubuf, snd, rcv, acc,
     rsb,
     lk, lw, xs, xr, zs, zr, ys, yr, ycs, ycr, qs, qr, qzs, qzr, qcs, qcr, os, orv, ocs, ocr, ss, rs, rss, rsr) = scratch[HEADS:]
    g = lax.axis_index("group")
    s = lax.axis_index("seq")
    y, c = g // 2, g % 2
    x, z = s // NZ, s % NZ
    factor = 1.0 / math.sqrt(HEAD)

    def at_y(yy):
        return {"group": lax.rem(yy + NY, NY) * 2 + c}

    def at_x(xx):
        return {"seq": lax.rem(xx + NX, NX) * NZ + z}

    def at_z(zz):
        return {"seq": x * NZ + lax.rem(zz + NZ, NZ)}

    partner = {"group": y * 2 + 1 - c}
    y_peer = (at_y(y + 1), at_y(y - 1))
    x_peer = (at_x(x + 1), at_x(x - 1))
    z_peer = (at_z(z + 1), at_z(z - 1))

    def remote(src, dst, send, recv, device):
        return pltpu.make_async_remote_copy(src, dst, send, recv, device_id=device, device_id_type=pl.DeviceIdType.MESH)

    def local_kv(h):
        return pltpu.make_async_copy(
            cache_ref.at[:, :, :, pl.ds(h * HEAD, HEAD)], kvs[h].at[:, :, x], lk.at[h]
        )

    has_queries = (y == 4) | (y == 5)
    my_rows = pl.ds(pl.multiple_of(z * ROWS, ROWS), ROWS)
    own_win = pltpu.make_async_copy(inw_ref, win.at[g], lw.at[0])
    own_part = pltpu.make_async_copy(inw_ref.at[my_rows, :], win.at[g, my_rows, :], lw.at[0])

    def own_weights(act):
        @pl.when(has_queries)
        def _():
            act(own_part)

        @pl.when(jnp.logical_not(has_queries))
        def _():
            act(own_win)

    own_wout = pltpu.make_async_copy(outw_ref, wout.at[g], lw.at[1])
    local_kv(0).start()
    local_kv(1).start()
    own_weights(lambda copy: copy.start())
    for h in range(2, HEADS):
        local_kv(h).start()
    own_wout.start()

    barrier = pltpu.get_barrier_semaphore()
    for peer in (partner,) + x_peer + tuple(at_y(y + k) for k in range(1, NY)) + tuple(at_z(z + k) for k in range(1, NZ)):
        pl.semaphore_signal(barrier, inc=1, device_id=peer, device_id_type=pl.DeviceIdType.MESH)

    for h in range(2):
        local_kv(h).wait()
    pl.semaphore_wait(barrier, 3 + NY - 1 + NZ - 1)

    def x_first(h, way):
        ref = kvs[h].at[:, :, x]
        return remote(ref, ref, xs.at[h, way], xr.at[h, way], x_peer[way])

    def x_second(h, way):
        block = lax.rem(x + (NX - 1 if way == 0 else 1), NX)
        ref = kvs[h].at[way, :, block]
        return remote(ref, ref, xs.at[h, 2 + way], xr.at[h, 2 + way], x_peer[way])

    def x_handle(h):
        for way in range(2):
            block = lax.rem(x + (NX - 1 if way == 0 else 1), NX)
            ref = kvs[h].at[:, :, block]
            remote(ref, ref, xs.at[h, way], xr.at[h, way], x_peer[way]).wait_recv()
            x_second(h, way).start()
        if h + WINDOW < HEADS:
            for way in range(2):
                x_first(h + WINDOW, way).start()

    def x_complete(h):
        block = lax.rem(x + 2, NX)
        for way in range(2):
            ref = kvs[h].at[way, :, block]
            remote(ref, ref, xs.at[h, 2 + way], xr.at[h, 2 + way], x_peer[way]).wait_recv()

    def z_copy(hop, part, way):
        block = lax.rem(z + (NZ - hop if way == 0 else hop), NZ)
        start = pl.multiple_of(block * ROWS + part * (ROWS // 2), ROWS // 2)
        ref = nbuf.at[pl.ds(start, ROWS // 2), :]
        return remote(ref, ref, zs.at[min(hop, 3), part, way], zr.at[min(hop, 3), part, way], z_peer[way])

    def z_arrival(hop, part, way):
        block = lax.rem(z + (NZ - hop if way == 0 else hop), NZ)
        start = pl.multiple_of(block * ROWS + part * (ROWS // 2), ROWS // 2)
        ref = nbuf.at[pl.ds(start, ROWS // 2), :]
        return remote(ref, ref, zs.at[hop - 1, part, way], zr.at[hop - 1, part, way], z_peer[way])

    def z_sends(hop, part, way):
        return hop < 3 or (hop == 3 and part == way)

    def z_handle(hop, part):
        for way in range(2):
            if hop < 4 or part == way:
                z_arrival(hop, part, way).wait_recv()
            if z_sends(hop, part, way):
                z_copy(hop, part, way).start()

    def w_ref(b, piece, core):
        return win.at[2 * b + core, pl.ds(piece * PIECE, PIECE), :]

    def y_block(way, hop):
        return lax.rem(y + NY - hop if way == 0 else y + hop, NY)

    def y_sends(way, hop, piece):
        return hop < 3 or (hop == 3 and piece == way)

    def y_copy(way, hop, piece):
        ref = w_ref(y_block(way, hop), piece, c)
        return remote(ref, ref, ys.at[way, hop, piece], yr.at[way, hop, piece], y_peer[way])

    def y_cross(b, piece):
        ref = w_ref(b, piece, c)
        return remote(ref, ref, ycs.at[b, piece], ycr.at[b, piece], partner)

    def y_cross_arrival(b):
        for piece in range(PIECES):
            ref = w_ref(b, piece, 1 - c)
            remote(ref, ref, ycs.at[b, piece], ycr.at[b, piece], partner).wait_recv()

    def y_guard(way, hop):
        b = y_block(way, hop)
        return (b != 4) & (b != 5)

    def y_slot(hop, piece):
        for way in range(2):
            if hop > 0 and not y_sends(way, hop - 1, piece):
                continue

            @pl.when(y_guard(way, hop))
            def _():
                b = y_block(way, hop)
                if hop > 0:
                    ref = w_ref(b, piece, c)
                    remote(ref, ref, ys.at[way, hop - 1, piece], yr.at[way, hop - 1, piece], y_peer[way]).wait_recv()
                if y_sends(way, hop, piece):
                    y_copy(way, hop, piece).start()
                if hop > 0 or way == 0:
                    y_cross(b, piece).start()

    def q_part(b, way, hop):
        block = lax.rem(z + NZ - hop if way == 0 else z + hop, NZ)
        if hop < 3:
            return win.at[2 * b + c, pl.ds(pl.multiple_of(block * ROWS, ROWS), ROWS), :]
        start = pl.multiple_of(block * ROWS + way * (ROWS // 2), ROWS // 2)
        return win.at[2 * b + c, pl.ds(start, ROWS // 2), :]

    def q_far(b, k):
        ref = win.at[2 * b + c, my_rows, :]
        return remote(ref, ref, qs.at[b - 4, k], qr.at[b - 4], at_y(y + k))

    def q_share():
        for b in (4, 5):
            @pl.when(y == b)
            def _():
                for k in (4, 3, 5, 2, 6, 1, 7):
                    q_far(b, k).start()

    def q_copy(b, hop, way):
        ref = q_part(b, way, hop)
        return remote(ref, ref, qzs.at[b - 4, hop, way], qzr.at[b - 4, hop, way], z_peer[way])

    def q_slot(hop):
        for b in (4, 5):
            if hop == 0:
                @pl.when(y != b)
                def _():
                    q_far(b, 1).wait_recv()

            for way in range(2):
                if hop > 0:
                    block = lax.rem(z + NZ - hop if way == 0 else z + hop, NZ)
                    if hop < 4:
                        ref = win.at[2 * b + c, pl.ds(pl.multiple_of(block * ROWS, ROWS), ROWS), :]
                    else:
                        start = pl.multiple_of(block * ROWS + way * (ROWS // 2), ROWS // 2)
                        ref = win.at[2 * b + c, pl.ds(start, ROWS // 2), :]
                    remote(ref, ref, qzs.at[b - 4, hop - 1, way], qzr.at[b - 4, hop - 1, way], z_peer[way]).wait_recv()
                if hop < 4:
                    q_copy(b, hop, way).start()
            if hop == 4:
                q_cross(b).start()

    def q_cross(b):
        ref = win.at[2 * b + c]
        return remote(ref, ref, qcs.at[b - 4], qcr.at[b - 4], partner)

    def q_cross_arrival(b):
        ref = win.at[2 * b + 1 - c]
        remote(ref, ref, qcs.at[b - 4], qcr.at[b - 4], partner).wait_recv()

    def o_copy(way, hop):
        ref = wout.at[2 * y_block(way, hop) + c]
        return remote(ref, ref, os.at[way, hop], orv.at[way, hop], y_peer[way])

    def o_cross(b):
        ref = wout.at[2 * b + c]
        return remote(ref, ref, ocs.at[b], ocr.at[b], partner)

    def o_slot(hop):
        for way in range(2):
            if hop == 4 and way == 1:
                continue
            b = y_block(way, hop)
            if hop > 0:
                ref = wout.at[2 * b + c]
                remote(ref, ref, os.at[way, hop - 1], orv.at[way, hop - 1], y_peer[way]).wait_recv()
            if hop < 3 or (hop == 3 and way == 0):
                o_copy(way, hop).start()
            if hop > 0 or way == 0:
                o_cross(b).start()

    def queries(block):
        @pl.loop(0, NZ // 2)
        def _(i):
            rows = pl.ds(pl.multiple_of(i * 2 * ROWS, 2 * ROWS), 2 * ROWS)
            value = jnp.dot(nbuf[rows, :], win[2 * 4 + block], preferred_element_type=jnp.float32)
            qbuf[rows, block * BLOCK : (block + 1) * BLOCK] = silu(value).astype(jnp.bfloat16)

    column = lax.broadcasted_iota(jnp.int32, (1, NX * SLOTS), 1)
    slot = (column // SLOTS * NZ + z) * SLOTS + column % SLOTS

    def send_partial(h, dest):
        return remote(snd.at[h, dest], rcv.at[h - RING, z], ss.at[h - RING, dest], rs.at[h - RING, z], at_z(dest))

    def attend(h):
        kv = kvs[h]

        def block(i):
            step = (i + 1) // 2
            dest = lax.rem(z + 4 + NZ + (1 - 2 * (i % 2)) * step, NZ)
            request = owner_ref[0, x * NZ + dest]
            length = len_ref[request]
            query = qbuf[pl.ds(pl.multiple_of(dest * ROWS, ROWS), ROWS), h * HEAD : (h + 1) * HEAD]
            keys = kv[0, request].reshape(NX * SLOTS, HEAD)
            values = kv[1, request].reshape(NX * SLOTS, HEAD)
            scores = lax.dot_general(
                query, keys, (((1,), (1,)), ((), ())), preferred_element_type=jnp.float32
            )
            weights = jnp.where(slot < length, silu(scores * factor), 0.0).astype(jnp.bfloat16)
            return dest, jnp.dot(weights, values, preferred_element_type=jnp.float32).astype(jnp.bfloat16)

        @pl.loop(0, NZ // UNROLL)
        def _(j):
            done = [block(j * UNROLL + k) for k in range(UNROLL)]
            for dest, part in done:
                snd[h, dest] = part
            if h >= RING:
                for k, (dest, _) in enumerate(done):
                    if k < UNROLL - 1:
                        send_partial(h, dest).start()
                    else:
                        @pl.when(j < NZ // UNROLL - 1)
                        def _():
                            send_partial(h, dest).start()

        if h < RING:
            ring_step(h, 1)
            pending[h] = 2

    def collect(h):
        total = acc[:, h * HEAD : (h + 1) * HEAD] + snd[h, z].astype(jnp.float32)
        for k in range(1, NZ):
            src = lax.rem(z + k, NZ)
            block = rcv.at[h - RING, src]
            remote(block, block, ss.at[h - RING, src], rs.at[h - RING, src], at_z(src)).wait_recv()
            total = total + rcv[h - RING, src].astype(jnp.float32)
        acc[:, h * HEAD : (h + 1) * HEAD] = total

    pending = {}

    def ring_rows(way, hop):
        return slice(0, ROWS) if hop > 1 else slice(0, ROWS // 2) if way == 0 else slice(ROWS // 2, ROWS)

    def ring_copy(h, hop, way):
        dest = lax.rem(z + 5 - hop if way == 0 else z + NZ - 5 + hop, NZ)
        rows = ring_rows(way, hop)
        return dest, remote(
            snd.at[h, dest, rows], rsb.at[way, h, hop - 1, rows], rss.at[way, h, hop - 1], rsr.at[way, h, hop - 1], z_peer[way]
        )

    def ring_take(h, hop, way):
        rows = ring_rows(way, hop)
        ref = rsb.at[way, h, hop - 1, rows]
        remote(ref, ref, rss.at[way, h, hop - 1], rsr.at[way, h, hop - 1], z_peer[way]).wait_recv()
        return rsb[way, h, hop - 1, rows].astype(jnp.float32)

    def ring_step(h, hop):
        for way in range(2):
            dest, copy = ring_copy(h, hop, way)
            if hop > 1:
                rows = ring_rows(way, hop - 1)
                total = snd[h, dest, rows].astype(jnp.float32) + ring_take(h, hop - 1, way)
                snd[h, dest, rows] = total.astype(jnp.bfloat16)
            copy.start()

    def tick():
        for h in sorted(pending):
            hop = pending[h]
            if hop <= 4:
                ring_step(h, hop)
                pending[h] = hop + 1
            else:
                columns = slice(h * HEAD, (h + 1) * HEAD)
                acc[:, columns] += snd[h, z].astype(jnp.float32) + ring_take(h, 4, 0) + ring_take(h, 4, 1)
                del pending[h]

    def own_rows():
        rows = pl.ds(pl.multiple_of(z * ROWS, ROWS), ROWS)
        mine = nbuf[rows, :]

        def project(block):
            value = jnp.dot(mine, win[block], preferred_element_type=jnp.float32)
            return silu(value).astype(jnp.bfloat16)

        for j in range(4):
            columns = slice(j * BLOCK, (j + 1) * BLOCK)
            ubuf[:, columns] = project(j)
            own_v = project(4 + j).astype(jnp.float32)
            own_k = project(12 + j).astype(jnp.float32)
            product = qbuf[rows, columns].astype(jnp.float32) * own_k
            for t in range(BLOCK // HEAD):
                part = slice(t * HEAD, (t + 1) * HEAD)
                score = jnp.sum(product[:, part], axis=-1, keepdims=True) * factor
                acc[:, j * BLOCK + t * HEAD : j * BLOCK + (t + 1) * HEAD] += silu(score) * own_v[:, part]

    own_weights(lambda copy: copy.wait())
    q_share()
    for h in range(2):
        for way in range(2):
            x_first(h, way).start()
    own_wout.wait()
    y_slot(0, 0)
    o_slot(0)
    nbuf[my_rows, :] = layer_norm(cand_ref[...].astype(jnp.float32), ing_ref[...]).astype(jnp.bfloat16)
    for part in range(2):
        for way in range(2):
            z_copy(0, part, way).start()
    acc[...] = jnp.zeros_like(acc)
    for h in range(2, HEADS):
        local_kv(h).wait()
    z_handle(1, 0)
    y_slot(0, 1)
    z_handle(1, 1)
    z_handle(2, 0)
    x_handle(0)
    q_slot(0)
    z_handle(2, 1)
    y_slot(1, 0)
    z_handle(3, 0)
    q_slot(1)
    z_handle(3, 1)
    x_handle(1)
    z_handle(4, 0)
    q_slot(2)
    y_slot(1, 1)
    z_handle(4, 1)
    q_slot(3)
    y_slot(2, 0)
    x_handle(2)
    q_slot(4)
    o_slot(1)
    y_slot(2, 1)
    q_cross_arrival(4)
    queries(0)
    queries(1)
    x_complete(0)
    attend(0)
    x_handle(3)
    y_slot(3, 0)
    o_slot(2)
    x_complete(1)
    tick()
    attend(1)
    q_cross_arrival(5)
    queries(2)
    queries(3)
    y_slot(3, 1)
    x_complete(2)
    tick()
    attend(2)
    x_handle(4)
    y_slot(4, 0)
    o_slot(3)
    x_complete(3)
    tick()
    attend(3)
    x_handle(5)
    y_slot(4, 1)
    x_complete(4)
    tick()
    attend(4)
    x_handle(6)
    o_slot(4)
    for b in range(NY):
        if b not in (4, 5):
            y_cross_arrival(b)
    own_rows()
    x_complete(5)
    tick()
    attend(5)
    tick()
    x_handle(7)
    for b in range(NY):
        remote(wout.at[2 * b + 1 - c], wout.at[2 * b + 1 - c], ocs.at[b], ocr.at[b], partner).wait_recv()
    tick()
    x_complete(6)
    tick()
    attend(6)
    tick()
    x_complete(7)
    attend(7)
    while pending:
        tick()
    for h in range(RING, HEADS):
        collect(h)
    gated = (layer_norm(acc[...], outg_ref[...]) * ubuf[...].astype(jnp.float32)).astype(jnp.bfloat16)
    result = jnp.dot(gated, wout[...].reshape(D, D), preferred_element_type=jnp.float32)
    out_ref[...] = (cand_ref[...].astype(jnp.float32) + result).astype(jnp.bfloat16)

    for h in range(HEADS):
        for way in range(2):
            x_first(h, way).wait_send()
            x_second(h, way).wait_send()
    for hop in range(4):
        for part in range(2):
            for way in range(2):
                if z_sends(hop, part, way):
                    z_copy(hop, part, way).wait_send()
    for way in range(2):
        for hop in range(4):
            @pl.when(y_guard(way, hop))
            def _():
                for piece in range(PIECES):
                    if y_sends(way, hop, piece):
                        y_copy(way, hop, piece).wait_send()

            if hop < 3 or way == 0:
                o_copy(way, hop).wait_send()
            for b in (4, 5):
                q_copy(b, hop, way).wait_send()
    for b in range(NY):
        o_cross(b).wait_send()
        if b in (4, 5):
            q_cross(b).wait_send()

            @pl.when(y == b)
            def _():
                for k in range(1, NY):
                    q_far(b, k).wait_send()
        else:
            for piece in range(PIECES):
                y_cross(b, piece).wait_send()
    for h in range(RING):
        for hop in range(1, 5):
            for way in range(2):
                ring_copy(h, hop, way)[1].wait_send()

    for h in range(RING, HEADS):
        @pl.loop(1, NZ)
        def _(k):
            send_partial(h, lax.rem(z + k, NZ)).wait_send()


def local(cand_x, in_weight, out_weight, in_gain, out_gain, cache_kv, hist_len, owner):
    bf16, dma = jnp.bfloat16, pltpu.SemaphoreType.DMA
    vmem, anywhere = pl.BlockSpec(memory_space=pltpu.VMEM), pl.BlockSpec(memory_space=pl.ANY)
    smem = pl.BlockSpec(memory_space=pltpu.SMEM)
    return pl.pallas_call(
        kernel,
        out_shape=jax.ShapeDtypeStruct((ROWS, D), bf16),
        in_specs=[vmem, anywhere, anywhere, vmem, vmem, anywhere, smem, smem],
        out_specs=vmem,
        scratch_shapes=[pltpu.VMEM((2, REQ, NX, SLOTS, HEAD), bf16) for _ in range(HEADS)]
        + [
            pltpu.VMEM((2 * NY, D, BLOCK), bf16),
            pltpu.VMEM((2 * NY, D // (2 * NY), D), bf16),
            pltpu.VMEM((NZ * ROWS, D), bf16),
            pltpu.VMEM((NZ * ROWS, D), bf16),
            pltpu.VMEM((ROWS, D), bf16),
            pltpu.VMEM((HEADS, NZ, ROWS, HEAD), bf16),
            pltpu.VMEM((max(HEADS - RING, 1), NZ, ROWS, HEAD), bf16),
            pltpu.VMEM((ROWS, D), jnp.float32),
            pltpu.VMEM((2, max(RING, 1), 4, ROWS, HEAD), bf16),
            dma((HEADS,)), dma((2,)),
            dma((HEADS, 4)), dma((HEADS, 4)),
            dma((4, 2, 2)), dma((4, 2, 2)),
            dma((2, 4, PIECES)), dma((2, 4, PIECES)), dma((NY, PIECES)), dma((NY, PIECES)),
            dma((2, NY)), dma((2,)), dma((2, 4, 2)), dma((2, 4, 2)), dma((2,)), dma((2,)),
            dma((2, 4)), dma((2, 4)), dma((NY,)), dma((NY,)),
            dma((max(HEADS - RING, 1), NZ)), dma((max(HEADS - RING, 1), NZ)),
            dma((2, max(RING, 1), 4)), dma((2, max(RING, 1), 4)),
        ],
        compiler_params=pltpu.CompilerParams(
            collective_id=0, has_side_effects=True, vmem_limit_bytes=56 * 1024 * 1024
        ),
        cost_estimate=pl.CostEstimate(flops=5_000_000_000, bytes_accessed=4_000_000, transcendentals=4_000_000),
    )(cand_x, in_weight, out_weight, in_gain[None, :], out_gain[None, :], cache_kv, hist_len, owner)


def solution(mesh):
    placed = (
        P(("group", "seq"), None),
        P(None, "group"),
        P("group", None),
        P(),
        P(),
        P(None, "group", "seq", None),
        P("group"),
        P("group", None),
    )
    return jax.shard_map(
        local, mesh=mesh, in_specs=placed, out_specs=P(("group", "seq"), None), check_vma=False
    )
```

time: 124 us -> 113 us (0.911)
  the two profiles are of different devices: /device:TPU:6 before, /device:TPU:8 now
where the time goes in v2:
time: 113 us
  Pallas kernels  112 us (99%)
  local copies, waits for them, and re-layouts  1.67 us (1%)
    pallas_call x1, Pallas kernels, local(): pl.pallas_call(kernel, out_shape=jax.ShapeDtypeStruct((ROWS, D), bf16), i...  112 us

profile of v2, /device:TPU:8, one launch (start us, length us, event | category | flops | bytes accessed | tf_op | source)
XLA Modules:
  0.0 113.2 jit_solution(5695506256769889051)
XLA Ops:
  0.0 111.5 %shard_map.82 = bf16[128,1024]{1,0:T(8,128)(2,1)} custom-call(bf16[128,1024]{1,0:T(8,128)(2,1)} %cand_ref.1, bf16[1024,256]{1,0:T(8,128)(2,1)} %inw_ref.1, bf16[64,1024]{1,0:T(8,128)(2,1)} %outw_ref.1, f32[1,1024]{1,0:T(1,128)} %bitcast.2, f32[1,1024]{1,0:T(1,128)} %bitcast.3, bf16[2,8,64,1024]{3,2,1,0:T(8,128)(2,1)} %cache_ref.1, s32[8]{0:T(128)} %len_ref.1, ...), custom_call_target="tpu_custom_call" | custom-call | flops 5000000000 | bytes 4000000 | tf_op jit(solution)/shard_map/pallas_call | solution.py:517
  111.5 1.7 %copy.10 = bf16[128,1024]{1,0:T(8,128)(2,1)} copy(bf16[128,1024]{1,0:T(8,128)(2,1)} %shard_map.82) | data formatting | bytes 524288

commit v3 on v2

--- a/solution.py
+++ b/solution.py
@@ -17,9 +17,9 @@
 SLOTS = 64
 REQ = 8
 PIECE = D // PIECES
-WINDOW = 2
+WINDOW = 3
 UNROLL = 2
-RING = 6
+RING = 2
 
 
 def silu(v):
@@ -34,9 +34,9 @@
     return centred * lax.rsqrt(spread + 1e-05) * gain
 
 
-def kernel(cand_ref, inw_ref, outw_ref, ing_ref, outg_ref, cache_ref, len_ref, owner_ref, out_ref, *scratch):
+def kernel(cand_hbm, inw_ref, outw_ref, ing_ref, outg_ref, cache_ref, len_ref, owner_ref, out_ref, *scratch):
     kvs = scratch[:HEADS]
-    (win, wout, nbuf, qbuf, ubuf, snd, rcv, acc,
+    (cand_ref, win, wout, nbuf, qbuf, ubuf, snd, rcv, acc,
      rsb,
      lk, lw, xs, xr, zs, zr, ys, yr, ycs, ycr, qs, qr, qzs, qzr, qcs, qcr, os, orv, ocs, ocr, ss, rs, rss, rsr) = scratch[HEADS:]
     g = lax.axis_index("group")
@@ -82,10 +82,11 @@
             act(own_win)
 
     own_wout = pltpu.make_async_copy(outw_ref, wout.at[g], lw.at[1])
+    own_rows_in = pltpu.make_async_copy(cand_hbm, cand_ref, lw.at[2])
     local_kv(0).start()
-    local_kv(1).start()
     own_weights(lambda copy: copy.start())
-    for h in range(2, HEADS):
+    own_rows_in.start()
+    for h in range(1, HEADS):
         local_kv(h).start()
     own_wout.start()
 
@@ -93,8 +94,7 @@
     for peer in (partner,) + x_peer + tuple(at_y(y + k) for k in range(1, NY)) + tuple(at_z(z + k) for k in range(1, NZ)):
         pl.semaphore_signal(barrier, inc=1, device_id=peer, device_id_type=pl.DeviceIdType.MESH)
 
-    for h in range(2):
-        local_kv(h).wait()
+    local_kv(0).wait()
     pl.semaphore_wait(barrier, 3 + NY - 1 + NZ - 1)
 
     def x_first(h, way):
@@ -106,19 +106,37 @@
         ref = kvs[h].at[way, :, block]
         return remote(ref, ref, xs.at[h, 2 + way], xr.at[h, 2 + way], x_peer[way])
 
+    def x_part(way, second):
+        index = 1 - way if second else way
+        ref = kvs[HEADS - 1].at[index, :, x]
+        return remote(ref, ref, xs.at[HEADS - 1, way + 4 * second], xr.at[HEADS - 1, way + 4 * second], x_peer[way])
+
+    def x_part_arrival(way, second):
+        index = 1 - way if second else way
+        block = lax.rem(x + (NX - 1 if way == 0 else 1), NX)
+        ref = kvs[HEADS - 1].at[index, :, block]
+        remote(ref, ref, xs.at[HEADS - 1, way + 4 * second], xr.at[HEADS - 1, way + 4 * second], x_peer[way]).wait_recv()
+
     def x_handle(h):
         for way in range(2):
-            block = lax.rem(x + (NX - 1 if way == 0 else 1), NX)
-            ref = kvs[h].at[:, :, block]
-            remote(ref, ref, xs.at[h, way], xr.at[h, way], x_peer[way]).wait_recv()
+            if h == HEADS - 1:
+                x_part_arrival(way, 0)
+            else:
+                block = lax.rem(x + (NX - 1 if way == 0 else 1), NX)
+                ref = kvs[h].at[:, :, block]
+                remote(ref, ref, xs.at[h, way], xr.at[h, way], x_peer[way]).wait_recv()
             x_second(h, way).start()
-        if h + WINDOW < HEADS:
-            for way in range(2):
+        for way in range(2):
+            if h + WINDOW < HEADS - 1:
                 x_first(h + WINDOW, way).start()
+            if h in (HEADS - 3, HEADS - 2):
+                x_part(way, h - (HEADS - 3)).start()
 
     def x_complete(h):
         block = lax.rem(x + 2, NX)
         for way in range(2):
+            if h == HEADS - 1:
+                x_part_arrival(way, 1)
             ref = kvs[h].at[way, :, block]
             remote(ref, ref, xs.at[h, 2 + way], xr.at[h, 2 + way], x_peer[way]).wait_recv()
 
@@ -208,26 +226,25 @@
         ref = q_part(b, way, hop)
         return remote(ref, ref, qzs.at[b - 4, hop, way], qzr.at[b - 4, hop, way], z_peer[way])
 
-    def q_slot(hop):
-        for b in (4, 5):
-            if hop == 0:
-                @pl.when(y != b)
-                def _():
-                    q_far(b, 1).wait_recv()
-
-            for way in range(2):
-                if hop > 0:
-                    block = lax.rem(z + NZ - hop if way == 0 else z + hop, NZ)
-                    if hop < 4:
-                        ref = win.at[2 * b + c, pl.ds(pl.multiple_of(block * ROWS, ROWS), ROWS), :]
-                    else:
-                        start = pl.multiple_of(block * ROWS + way * (ROWS // 2), ROWS // 2)
-                        ref = win.at[2 * b + c, pl.ds(start, ROWS // 2), :]
-                    remote(ref, ref, qzs.at[b - 4, hop - 1, way], qzr.at[b - 4, hop - 1, way], z_peer[way]).wait_recv()
+    def q_slot(b, hop):
+        if hop == 0:
+            @pl.when(y != b)
+            def _():
+                q_far(b, 1).wait_recv()
+
+        for way in range(2):
+            if hop > 0:
+                block = lax.rem(z + NZ - hop if way == 0 else z + hop, NZ)
                 if hop < 4:
-                    q_copy(b, hop, way).start()
-            if hop == 4:
-                q_cross(b).start()
+                    ref = win.at[2 * b + c, pl.ds(pl.multiple_of(block * ROWS, ROWS), ROWS), :]
+                else:
+                    start = pl.multiple_of(block * ROWS + way * (ROWS // 2), ROWS // 2)
+                    ref = win.at[2 * b + c, pl.ds(start, ROWS // 2), :]
+                remote(ref, ref, qzs.at[b - 4, hop - 1, way], qzr.at[b - 4, hop - 1, way], z_peer[way]).wait_recv()
+            if hop < 4:
+                q_copy(b, hop, way).start()
+        if hop == 4:
+            q_cross(b).start()
 
     def q_cross(b):
         ref = win.at[2 * b + c]
@@ -374,102 +391,116 @@
 
     own_weights(lambda copy: copy.wait())
     q_share()
-    for h in range(2):
-        for way in range(2):
-            x_first(h, way).start()
+    for way in range(2):
+        x_first(0, way).start()
     own_wout.wait()
     y_slot(0, 0)
     o_slot(0)
+    own_rows_in.wait()
     nbuf[my_rows, :] = layer_norm(cand_ref[...].astype(jnp.float32), ing_ref[...]).astype(jnp.bfloat16)
     for part in range(2):
         for way in range(2):
             z_copy(0, part, way).start()
+    local_kv(1).wait()
+    for way in range(2):
+        x_first(1, way).start()
     acc[...] = jnp.zeros_like(acc)
     for h in range(2, HEADS):
         local_kv(h).wait()
+    for way in range(2):
+        x_first(2, way).start()
+    y_slot(0, 1)
     z_handle(1, 0)
-    y_slot(0, 1)
     z_handle(1, 1)
+    q_slot(4, 0)
+    x_handle(0)
     z_handle(2, 0)
-    x_handle(0)
-    q_slot(0)
     z_handle(2, 1)
     y_slot(1, 0)
+    q_slot(4, 1)
+    q_slot(4, 2)
+    y_slot(1, 1)
+    x_handle(1)
     z_handle(3, 0)
-    q_slot(1)
     z_handle(3, 1)
-    x_handle(1)
+    q_slot(4, 3)
+    q_slot(5, 0)
     z_handle(4, 0)
-    q_slot(2)
-    y_slot(1, 1)
     z_handle(4, 1)
-    q_slot(3)
+    q_slot(4, 4)
+    q_slot(5, 1)
     y_slot(2, 0)
     x_handle(2)
-    q_slot(4)
-    o_slot(1)
-    y_slot(2, 1)
+    q_slot(5, 2)
     q_cross_arrival(4)
     queries(0)
-    queries(1)
     x_complete(0)
     attend(0)
-    x_handle(3)
-    y_slot(3, 0)
-    o_slot(2)
+    q_slot(5, 3)
+    y_slot(2, 1)
+    queries(1)
     x_complete(1)
     tick()
     attend(1)
+    q_slot(5, 4)
+    x_handle(3)
+    y_slot(3, 0)
+    x_complete(2)
+    tick()
+    attend(2)
+    o_slot(1)
     q_cross_arrival(5)
     queries(2)
     queries(3)
     y_slot(3, 1)
-    x_complete(2)
-    tick()
-    attend(2)
     x_handle(4)
-    y_slot(4, 0)
-    o_slot(3)
     x_complete(3)
     tick()
     attend(3)
+    o_slot(2)
+    y_slot(4, 0)
+    y_slot(4, 1)
     x_handle(5)
-    y_slot(4, 1)
     x_complete(4)
     tick()
     attend(4)
-    x_handle(6)
-    o_slot(4)
+    o_slot(3)
     for b in range(NY):
         if b not in (4, 5):
             y_cross_arrival(b)
     own_rows()
+    o_slot(4)
+    x_handle(6)
     x_complete(5)
     tick()
     attend(5)
-    tick()
     x_handle(7)
+    for h in range(RING, 5):
+        collect(h)
     for b in range(NY):
         remote(wout.at[2 * b + 1 - c], wout.at[2 * b + 1 - c], ocs.at[b], ocr.at[b], partner).wait_recv()
-    tick()
     x_complete(6)
-    tick()
     attend(6)
     tick()
+    collect(5)
     x_complete(7)
     attend(7)
     while pending:
         tick()
-    for h in range(RING, HEADS):
-        collect(h)
+    collect(6)
+    collect(7)
     gated = (layer_norm(acc[...], outg_ref[...]) * ubuf[...].astype(jnp.float32)).astype(jnp.bfloat16)
     result = jnp.dot(gated, wout[...].reshape(D, D), preferred_element_type=jnp.float32)
     out_ref[...] = (cand_ref[...].astype(jnp.float32) + result).astype(jnp.bfloat16)
 
     for h in range(HEADS):
         for way in range(2):
-            x_first(h, way).wait_send()
             x_second(h, way).wait_send()
+            if h < HEADS - 1:
+                x_first(h, way).wait_send()
+            else:
+                x_part(way, 0).wait_send()
+                x_part(way, 1).wait_send()
     for hop in range(4):
         for part in range(2):
             for way in range(2):
@@ -517,10 +548,11 @@
     return pl.pallas_call(
         kernel,
         out_shape=jax.ShapeDtypeStruct((ROWS, D), bf16),
-        in_specs=[vmem, anywhere, anywhere, vmem, vmem, anywhere, smem, smem],
+        in_specs=[anywhere, anywhere, anywhere, vmem, vmem, anywhere, smem, smem],
         out_specs=vmem,
         scratch_shapes=[pltpu.VMEM((2, REQ, NX, SLOTS, HEAD), bf16) for _ in range(HEADS)]
         + [
+            pltpu.VMEM((ROWS, D), bf16),
             pltpu.VMEM((2 * NY, D, BLOCK), bf16),
             pltpu.VMEM((2 * NY, D // (2 * NY), D), bf16),
             pltpu.VMEM((NZ * ROWS, D), bf16),
@@ -530,8 +562,8 @@
             pltpu.VMEM((max(HEADS - RING, 1), NZ, ROWS, HEAD), bf16),
             pltpu.VMEM((ROWS, D), jnp.float32),
             pltpu.VMEM((2, max(RING, 1), 4, ROWS, HEAD), bf16),
-            dma((HEADS,)), dma((2,)),
-            dma((HEADS, 4)), dma((HEADS, 4)),
+            dma((HEADS,)), dma((3,)),
+            dma((HEADS, 6)), dma((HEADS, 6)),
             dma((4, 2, 2)), dma((4, 2, 2)),
             dma((2, 4, PIECES)), dma((2, 4, PIECES)), dma((NY, PIECES)), dma((NY, PIECES)),
             dma((2, NY)), dma((2,)), dma((2, 4, 2)), dma((2, 4, 2)), dma((2,)), dma((2,)),

time: 113 us -> 105 us (0.929)
  the two profiles are of different devices: /device:TPU:8 before, /device:TPU:6 now
where the time goes in v3:
time: 105 us
  Pallas kernels  103 us (98%)
  local copies, waits for them, and re-layouts  1.67 us (2%)
    pallas_call x1, Pallas kernels, local(): pl.pallas_call(kernel, out_shape=jax.ShapeDtypeStruct((ROWS, D), bf16), i...  103 us

profile of v3, /device:TPU:6, one launch (start us, length us, event | category | flops | bytes accessed | tf_op | source)
XLA Modules:
  0.0 104.8 jit_solution(16935585818178857188)
XLA Ops:
  0.0 103.1 %shard_map.82 = bf16[128,1024]{1,0:T(8,128)(2,1)} custom-call(bf16[128,1024]{1,0:T(8,128)(2,1)} %cand_hbm.1, bf16[1024,256]{1,0:T(8,128)(2,1)} %inw_ref.1, bf16[64,1024]{1,0:T(8,128)(2,1)} %outw_ref.1, f32[1,1024]{1,0:T(1,128)} %bitcast.2, f32[1,1024]{1,0:T(1,128)} %bitcast.3, bf16[2,8,64,1024]{3,2,1,0:T(8,128)(2,1)} %cache_ref.1, s32[8]{0:T(128)} %len_ref.1, ...), custom_call_target="tpu_custom_call" | custom-call | flops 5000000000 | bytes 4000000 | tf_op jit(solution)/shard_map/pallas_call | solution.py:548
  103.1 1.7 %copy.10 = bf16[128,1024]{1,0:T(8,128)(2,1)} copy(bf16[128,1024]{1,0:T(8,128)(2,1)} %shard_map.82) | data formatting | bytes 524288

commit v4 on v3

--- a/solution.py
+++ b/solution.py
@@ -62,6 +62,15 @@
     def remote(src, dst, send, recv, device):
         return pltpu.make_async_remote_copy(src, dst, send, recv, device_id=device, device_id_type=pl.DeviceIdType.MESH)
 
+    barrier = pltpu.get_barrier_semaphore()
+    for peer in (partner,) + x_peer + y_peer + tuple(at_z(z + k) for k in range(1, NZ)):
+        pl.semaphore_signal(barrier, inc=1, device_id=peer, device_id_type=pl.DeviceIdType.MESH)
+
+    for b in (4, 5):
+        @pl.when((y < b - 1) | (y > b + 1))
+        def _():
+            pl.semaphore_signal(barrier, inc=1, device_id=at_y(b), device_id_type=pl.DeviceIdType.MESH)
+
     def local_kv(h):
         return pltpu.make_async_copy(
             cache_ref.at[:, :, :, pl.ds(h * HEAD, HEAD)], kvs[h].at[:, :, x], lk.at[h]
@@ -90,12 +99,8 @@
         local_kv(h).start()
     own_wout.start()
 
-    barrier = pltpu.get_barrier_semaphore()
-    for peer in (partner,) + x_peer + tuple(at_y(y + k) for k in range(1, NY)) + tuple(at_z(z + k) for k in range(1, NZ)):
-        pl.semaphore_signal(barrier, inc=1, device_id=peer, device_id_type=pl.DeviceIdType.MESH)
-
     local_kv(0).wait()
-    pl.semaphore_wait(barrier, 3 + NY - 1 + NZ - 1)
+    pl.semaphore_wait(barrier, jnp.where((y == 4) | (y == 5), 3 + NY - 1 + NZ - 1, 5 + NZ - 1))
 
     def x_first(h, way):
         ref = kvs[h].at[:, :, x]

time: 105 us -> 104 us (level)
    pallas_call x1, Pallas kernels: 103 us -> 102 us  [local(): pl.pallas_call(kernel, out_shape=jax.ShapeDtypeStruct((ROWS, D), bf16), i...]
where the time goes in v4:
time: 104 us; the launch traced here: 103 us
  Pallas kernels  102 us (98%)
  local copies, waits for them, and re-layouts  1.67 us (2%)
    pallas_call x1, Pallas kernels, local(): pl.pallas_call(kernel, out_shape=jax.ShapeDtypeStruct((ROWS, D), bf16), i...  102 us

profile of v4, /device:TPU:6, one launch (start us, length us, event | category | flops | bytes accessed | tf_op | source)
XLA Modules:
  0.0 103.5 jit_solution(13642814602165309942)
XLA Ops:
  0.0 101.8 %shard_map.82 = bf16[128,1024]{1,0:T(8,128)(2,1)} custom-call(bf16[128,1024]{1,0:T(8,128)(2,1)} %cand_hbm.1, bf16[1024,256]{1,0:T(8,128)(2,1)} %inw_ref.1, bf16[64,1024]{1,0:T(8,128)(2,1)} %outw_ref.1, f32[1,1024]{1,0:T(1,128)} %bitcast.2, f32[1,1024]{1,0:T(1,128)} %bitcast.3, bf16[2,8,64,1024]{3,2,1,0:T(8,128)(2,1)} %cache_ref.1, s32[8]{0:T(128)} %len_ref.1, ...), custom_call_target="tpu_custom_call" | custom-call | flops 5000000000 | bytes 4000000 | tf_op jit(solution)/shard_map/pallas_call | solution.py:553
  101.8 1.7 %copy.10 = bf16[128,1024]{1,0:T(8,128)(2,1)} copy(bf16[128,1024]{1,0:T(8,128)(2,1)} %shard_map.82) | data formatting | bytes 524288
